TPU v7x, 512 devices: a whole 4x8x8 slice. The times are simulated.
512 devices in a mesh: dp: 32 (over z, x_lo, core), expert: 16 (over x_hi, y).
Axes of the slice: x: 4 (x_hi: 2, x_lo: 2; x = x_hi * 2 + x_lo), y: 8, z: 8, core: 2. Of those that a mesh axis runs over, the one named last changes fastest.
Arguments:
- tokens: bfloat16 [1536, 4096], P(('dp', 'expert')), may hold values from -6 to 6
- expert_ids: int32 [1536, 8], P('dp'), may hold values from 0 to 63, all different within a row; in each aligned block of 48 rows (0 to 47, 48 to 95, ...) at most 10 rows name the same one
- gate_ints: int32 [1536, 8], P('dp'), may hold values from 1024 to 65535
- gate_weight: bfloat16 [512, 192, 4096], P(('expert', 'dp')), may hold values from -0.09375 to 0.09375
- up_weight: bfloat16 [512, 192, 4096], P(('expert', 'dp')), may hold values from -0.09375 to 0.09375
- down_weight: bfloat16 [512, 192, 4096], P(('expert', 'dp')), may hold values from -0.15625 to 0.15625
Outputs:
- mixed: bfloat16 [1536, 4096], P(('dp', 'expert'))
Inputs may be any that keep to these rules, and one draw needn't show every extreme that they name: `expert_ids`: each row names 8 different experts. Among the 48 rows of one index of dp (aligned blocks), no expert is named by more than 10 rows, a bound that some block reaches.
All inputs are finite; a program needn't handle non-finite values.
Results may differ from a plain program's by a relative error of at most 0.02.
Values may be sent and summed in bfloat16 or wider, within the bound.
A program may use at most 64 MiB of HBM per device.

v0:
```python
import jax
import jax.numpy as jnp
from jax import lax
from jax.sharding import PartitionSpec as P

SLICES = 8


def expert_rows(rows, w_gate, w_up, w_down):
    flat_rows = rows.reshape(-1, rows.shape[-1])
    contract = (((1,), (1,)), ((), ()))
    gate_proj = lax.dot_general(flat_rows, w_gate, contract, preferred_element_type=jnp.float32)
    up_proj = lax.dot_general(flat_rows, w_up, contract, preferred_element_type=jnp.float32)
    hidden = (jax.nn.silu(gate_proj) * up_proj).astype(jnp.bfloat16)
    partial_value = jnp.dot(hidden, w_down, preferred_element_type=jnp.float32).astype(jnp.bfloat16)
    return partial_value.reshape(rows.shape[:-1] + (w_down.shape[1],))


def local(tokens, expert_ids, gate_ints, gate_weight, up_weight, down_weight):
    dp_count = lax.axis_size("dp")
    groups = dp_count // SLICES
    experts = lax.axis_size("expert") * groups
    block_rows = expert_ids.shape[0]
    per_token = expert_ids.shape[1]
    capacity = 5 * block_rows * per_token // (3 * experts)
    gathered = lax.all_gather(tokens, "expert", axis=0, tiled=True)
    model_width = gathered.shape[1]
    column = lax.axis_index("expert")
    shares = gate_ints.astype(jnp.float32)
    shares = shares / jnp.sum(shares, axis=1, keepdims=True)
    flat_ids = expert_ids.reshape(-1)
    in_column = flat_ids // groups == column
    group_of = flat_ids % groups
    onehot = (
        (group_of[:, None] == jnp.arange(groups, dtype=jnp.int32)[None, :]) & in_column[:, None]
    ).astype(jnp.int32)
    before = jnp.cumsum(onehot, axis=0) - onehot
    order_rank = jnp.sum(before * onehot, axis=1)
    slot_index = jnp.where(in_column, group_of * capacity + order_rank, -1)
    slot_table = slot_index.reshape(block_rows, per_token)
    targets = jnp.arange(groups * capacity, dtype=jnp.int32)
    placement = jnp.any(slot_table[None, :, :] == targets[:, None, None], axis=2)
    send_rows = jnp.dot(
        placement.astype(jnp.bfloat16), gathered, preferred_element_type=jnp.float32
    )
    send_rows = send_rows.astype(jnp.bfloat16).reshape(groups, capacity, model_width)
    w_gate = gate_weight[0]
    w_up = up_weight[0]
    w_down = down_weight[0]
    my_group = lax.axis_index("dp") // SLICES
    picked = lax.dynamic_index_in_dim(
        lax.all_gather(send_rows[None], "dp", axis=0, tiled=True), my_group, 1, keepdims=False
    )
    parts = expert_rows(picked, w_gate, w_up, w_down)
    returned = lax.all_to_all(parts, "dp", split_axis=0, concat_axis=0, tiled=True)
    summed = jnp.sum(
        returned.reshape(groups, SLICES, capacity, model_width).astype(jnp.float32), axis=1
    )
    summed = summed.reshape(groups * capacity, model_width)
    weights_table = jnp.sum(
        jnp.where(
            slot_table[:, :, None] == targets[None, None, :],
            shares[:, :, None],
            jnp.zeros((), jnp.float32),
        ),
        axis=1,
    )
    column_out = jnp.dot(
        weights_table, summed, precision=lax.Precision.HIGHEST, preferred_element_type=jnp.float32
    )
    mixed = lax.psum_scatter(
        column_out.astype(jnp.bfloat16), "expert", scatter_dimension=0, tiled=True
    )
    return mixed


def solution(mesh):
    return jax.shard_map(
        local,
        mesh=mesh,
        in_specs=(
            P(("dp", "expert"), None),
            P("dp", None),
            P("dp", None),
            P(("expert", "dp"), None, None),
            P(("expert", "dp"), None, None),
            P(("expert", "dp"), None, None),
        ),
        out_specs=P(("dp", "expert"), None),
        check_vma=False,
    )
```

profile of v0, /device:TPU:1, one launch (start us, length us, event | category | flops | bytes accessed | tf_op | source)
XLA Modules:
  0.0 433.1 jit_solution(9094356615377154165)
XLA Ops:
  6.5 0.9 copy.25
  7.4 0.1 reshape.167
  7.7 1.2 reduce-window.6
  8.9 0.2 slice_reduce_fusion
  9.1 0.2 reduce-window.9
  9.7 38.1 %all-gather = bf16[16,3,4096]{2,1,0:T(4,128)(2,1)S(1)} all-gather(bf16[1,3,4096]{2,1,0:T(4,128)(2,1)} %bitcast.45), channel_id=1, replica_groups=mesh['dp'=32,'expert'=16] {'expert'}, dimensions={0}, use_global_device_ids=true | all-gather | bytes 417792 | tf_op jit(solution)/shard_map/all_gather | solution.py:26
  47.8 0.3 reshape.174
  48.1 0.2 convolution_convert_fusion.2
  48.3 0.1 broadcast_in_dim_reshape.2
  48.5 1.0 copy.33
  49.5 83.4 %all-gather.3.cloned.1.call-done = bf16[32,4,10,4096]{3,1,2,0:T(4,128)(2,1)} async-done(((bf16[1,4,10,4096]{3,1,2,0:T(4,128)(2,1)}), bf16[32,4,10,4096]{3,1,2,0:T(4,128)(2,1)}) %all-gather.3.cloned.1.call-update) | async-done | bytes 10485776 | tf_op jit(solution)/shard_map/all_gather | solution.py:52
  132.9 19.5 %dynamic-slice_reduce_fusion = bf16[32,10,4096]{2,1,0:T(8,128)(2,1)} fusion(bf16[32,4,10,4096]{3,1,2,0:T(4,128)(2,1)} %all-gather.3.cloned.1.call-done, s32[]{:T(128)S(6)} %select_n.67), kind=kLoop, calls=%fused_computation.2 | loop fusion | bytes 5242884 | tf_op jit(solution)/shard_map/jit(dynamic_index_in_dim)/dynamic_slice | solution.py:51
  152.4 4.7 %reshape.169 = bf16[320,4096]{1,0:T(8,128)(2,1)} reshape(bf16[32,10,4096]{2,1,0:T(8,128)(2,1)} %dynamic-slice_reduce_fusion) | data formatting | bytes 5242880 | tf_op jit(solution)/shard_map/reshape | solution.py:10
  157.1 3.4 fusion.3
  160.5 6.0 %convolution_convert_fusion = bf16[320,4096]{1,0:T(8,128)(2,1)} fusion(bf16[1,192,4096]{2,1,0:T(8,128)(2,1)S(1)} %copy-done, bf16[320,4096]{1,0:T(8,128)(2,1)} %reshape.169, bf16[1,192,4096]{2,1,0:T(8,128)(2,1)} %param.10, f32[320,192]{0,1:T(8,128)S(1)} %fusion.3), kind=kOutput, calls=%fused_computation.1 | convolution fusion | flops 1008312320 | bytes 8634368 | tf_op jit(solution)/shard_map/dot_general | solution.py:15
  166.5 4.6 %reshape.170 = bf16[32,10,4096]{2,1,0:T(8,128)(2,1)} reshape(bf16[320,4096]{1,0:T(8,128)(2,1)} %convolution_convert_fusion) | data formatting | bytes 5242880 | tf_op jit(solution)/shard_map/reshape | solution.py:16
  171.2 5.6 %all-to-all-start = ((bf16[32,10,4096]{2,1,0:T(8,128)(2,1)}), bf16[32,10,4096]{2,1,0:T(8,128)(2,1)}, u32[]{:S(2)}, u32[]{:S(2)}) async-start(bf16[32,10,4096]{2,1,0:T(8,128)(2,1)} %reshape.170), calls=%async_computation | async-start | bytes 8388608 | tf_op jit(solution)/shard_map/all_to_all | solution.py:55
  176.9 94.0 %all-to-all-done = bf16[32,10,4096]{2,1,0:T(8,128)(2,1)} async-done(((bf16[32,10,4096]{2,1,0:T(8,128)(2,1)}), bf16[32,10,4096]{2,1,0:T(8,128)(2,1)}, u32[]{:S(2)}, u32[]{:S(2)}) %all-to-all-start) | async-done | bytes 2621472 | tf_op jit(solution)/shard_map/all_to_all | solution.py:55
  270.9 3.0 convert_reduce_fusion
  273.9 0.1 reshape.171
  274.0 1.6 convolution_convert_fusion.1
  275.6 1.3 dynamic-slice
  277.5 147.2 %all-reduce.3.cloned.1.call-done = bf16[48,4096]{1,0:T(8,128)(2,1)} async-done(((bf16[48,4096]{1,0:T(8,128)(2,1)}), bf16[48,4096]{1,0:T(8,128)(2,1)}) %all-reduce.3.cloned.1.call-update) | async-done | bytes 393232
  424.7 1.5 constant_dynamic-slice_fusion
  (23 shorter events, 0.6 us)
Async XLA Ops:
  6.5 154.0 %copy-start = (bf16[1,192,4096]{2,1,0:T(8,128)(2,1)S(1)}, bf16[1,192,4096]{2,1,0:T(8,128)(2,1)}, u32[]{:S(2)}) copy-start(bf16[1,192,4096]{2,1,0:T(8,128)(2,1)} %param.11) | copy-start | bytes 4718596
  6.5 126.4 %all-gather.3.cloned.1.call-start = ((), (), s32[]{:S(2)}) async-start(), calls=%async_computation.1 | async-start | bytes 10813440 | tf_op jit(solution)/shard_map/all_gather | solution.py:52
  171.2 5.7 %copy-start.1 = (s32[48,8]{0,1:T(8,128)S(1)}, s32[48,8]{0,1:T(8,128)}, u32[]{:S(2)}) copy-start(s32[48,8]{0,1:T(8,128)} %param.8) | copy-start | bytes 4612
  171.2 99.7 %all-to-all-start = ((bf16[32,10,4096]{2,1,0:T(8,128)(2,1)}), bf16[32,10,4096]{2,1,0:T(8,128)(2,1)}, u32[]{:S(2)}, u32[]{:S(2)}) async-start(bf16[32,10,4096]{2,1,0:T(8,128)(2,1)} %reshape.170), calls=%async_computation | async-start | bytes 8388608 | tf_op jit(solution)/shard_map/all_to_all | solution.py:55
  176.8 247.9 %all-reduce.3.cloned.1.call-start = ((), (), s32[]{:S(2)}) async-start(), calls=%async_computation.2 | async-start | bytes 786432
Sparse Core Ops, SparseCore 0:
  49.6 83.2 all-gather.2
  275.7 148.9 all-reduce.2
where the time goes:
time: 442 us; the launch traced here: 433 us
  waiting for transfers between devices  325 us (74%)
  blocking collectives  38.1 us (9%)
  local copies, waits for them, and re-layouts  34.6 us (8%)
  between operations  14.2 us (3%)
  matrix products  11.2 us (3%)
  starting transfers between devices  5.69 us (1%)
  other arithmetic  4.75 us (1%)
    unnamed x3, waiting for transfers between devices  147 us
    all_to_all x1, waiting for transfers between devices, local(): lax.all_to_all(parts, 'dp', split_axis=0, concat_axis=0, tiled=True)  94 us
    all_gather x1, waiting for transfers between devices, local(): lax.all_gather(send_rows[None], 'dp', axis=0, tiled=True)  83.4 us
    all_gather x1, blocking collectives, local(): gathered = lax.all_gather(tokens, 'expert', axis=0, tiled=True)  38.1 us
    dynamic_slice x1, local copies, waits for them, and re-layouts, local(): lax.dynamic_index_in_dim(lax.all_gather(send_rows[None], 'dp', axis=0, ti...  19.5 us
  transfers between devices with their start and end apart: 3, of which 3 were waited for; matrix products, arithmetic and copies ran while one was open for 0% of the time, Pallas kernels for 0%

commit v1 on v0

v1 whole, which is shorter than its diff:
```python
import functools

import jax
import jax.numpy as jnp
from jax import lax
from jax.experimental import pallas as pl
from jax.experimental.pallas import tpu as pltpu
from jax.sharding import PartitionSpec as P

SLICES = 8
CAP = 10
BF = jnp.bfloat16
F32 = jnp.float32
HIGH = lax.Precision.HIGHEST


def quotient(x, n, top):
    mul = (1 << 16) // n + 1
    assert all((v * mul) >> 16 == v // n for v in range(top))
    return (x * mul) >> 16


def iota(shape, dim):
    return lax.broadcasted_iota(jnp.int32, shape, dim)


def dot32(a, b):
    return jnp.dot(a, b, preferred_element_type=F32)


def dot_rows(a, b):
    return lax.dot_general(a, b, (((1,), (1,)), ((), ())), preferred_element_type=F32)


def kernel(
    sizes, tokens_ref, ids_ref, gates_ref, wg_hbm, wu_hbm, wd_hbm, out_ref,
    wg, wu, wd, stage32, stage, a0r, tabs, blk, gath, pick, sel, xb, acc, hid,
    pcs, pcr, xs, xr, own, zs, zr, rl, rls, mixw, es32, es, er, fin, finr,
    wsem, a0s, a0q, tbs, tbq, a1s, a1q, bzs, bzq, brs, bxs, bxq, bcs, bcq,
    dcs, dcq, dxs, dxq, dzs, dzq, rss, rsq, e1s, e1q, e2s, e2q,
):
    cols, groups, own_rows, width, hidden = sizes
    zn = 2 * groups
    sw = width // SLICES
    hw = sw // 2
    qn = sw // 128
    block = 2 * SLICES * own_rows
    half = SLICES * own_rows
    slots = SLICES * CAP
    lanes = cols * block
    ring8 = zn == 8

    d = lax.axis_index("dp")
    c = lax.axis_index("expert")
    g = lax.div(d, SLICES)
    i = lax.rem(d, SLICES)
    zb = lax.div(i, 4)
    xl = lax.rem(lax.div(i, 2), 2)
    core = lax.rem(i, 2)
    z = 2 * g + zb
    p = xl * 2 + core
    px = (1 - xl) * 2 + core

    def at_cube(j):
        return {"dp": g * SLICES + j, "expert": c}

    def at_column(k):
        return {"dp": d, "expert": k}

    def at_z(k):
        return {"dp": k * 4 + p, "expert": c}

    x_mate = {"dp": z * 4 + px, "expert": c}
    core_mate = {"dp": z * 4 + xl * 2 + (1 - core), "expert": c}
    z_mate_z = 2 * g + (1 - zb)

    def remote(src, dst, ssem, rsem, dev):
        return pltpu.make_async_remote_copy(
            src_ref=src, dst_ref=dst, send_sem=ssem, recv_sem=rsem,
            device_id=dev, device_id_type=pl.DeviceIdType.MESH,
        )

    loads = [
        pltpu.make_async_copy(wg_hbm.at[0], wg, wsem.at[0]),
        pltpu.make_async_copy(wu_hbm.at[0], wu, wsem.at[1]),
        pltpu.make_async_copy(wd_hbm.at[0], wd, wsem.at[2]),
    ]
    for load in loads:
        load.start()

    barrier = pltpu.get_barrier_semaphore()

    def signal(dev):
        pl.semaphore_signal(barrier, inc=1, device_id=dev, device_id_type=pl.DeviceIdType.MESH)

    for k in range(1, SLICES):
        signal(at_cube(lax.rem(i + k, SLICES)))
    for k in range(1, cols):
        signal(at_column(lax.rem(c + k, cols)))
    for k in range(1, groups):
        other = lax.rem(g + k, groups)
        signal(at_z(2 * other))
        signal(at_z(2 * other + 1))

    tok = tokens_ref[...].astype(F32)
    stage32[...] = jnp.zeros_like(stage32)
    for k in range(SLICES * qn):
        stage32[4 * k : 4 * k + own_rows, :] = tok[:, 128 * k : 128 * (k + 1)]
    stage[...] = stage32[...].astype(BF).reshape(stage.shape)

    ids = ids_ref[...]
    gates = gates_ref[...].astype(F32)
    shares = gates / jnp.sum(gates, axis=1, keepdims=True)
    rows = ids.shape[0]
    lane = iota((rows, 128), 1)
    cat = jnp.zeros((rows, 128), F32)
    for k in range(groups):
        hit = ids == c * groups + k
        named = jnp.sum(jnp.where(hit, 1.0, 0.0), axis=1, keepdims=True)
        weight = jnp.sum(jnp.where(hit, shares, 0.0), axis=1, keepdims=True)
        cat = jnp.where(lane == k, named, cat)
        cat = jnp.where(lane == 4 + k, weight, cat)
    lower = jnp.where(iota((rows, rows), 1) < iota((rows, rows), 0), 1.0, 0.0)
    rank = dot32(lower.astype(BF), cat.astype(BF))
    base = (i * CAP + 1).astype(F32)
    table = jnp.where(lane < 4, jnp.where(cat > 0.0, rank + base, 0.0), cat)
    table = jnp.concatenate([table, jnp.zeros((128 - rows, 128), F32)], axis=0)
    tabs[i] = jnp.transpose(table)[0:8, :]
    a0r[i] = stage[i]

    pl.semaphore_wait(barrier, SLICES - 1 + cols - 1 + zn - 2)

    def slice_copy(j):
        return remote(stage.at[j], a0r.at[i], a0s.at[j], a0q.at[i], at_cube(j))

    def table_copy(j):
        return remote(tabs.at[i], tabs.at[i], tbs.at[j], tbq.at[i], at_cube(j))

    for k in range(1, SLICES):
        slice_copy(lax.rem(i + k, SLICES)).start()
    for k in range(1, SLICES):
        table_copy(lax.rem(i + k, SLICES)).start()
    for k in range(1, SLICES):
        j = lax.rem(i + k, SLICES)
        remote(stage.at[j], a0r.at[j], a0s.at[j], a0q.at[j], at_cube(j)).wait_recv()

    flat = a0r[...].reshape(SLICES * 16, 128)
    row = iota((block, SLICES * 16), 0)
    hrow = jnp.where(row >= half, 1, 0)
    rem = row - half * hrow
    dpr = quotient(rem, own_rows, half)
    tgt = dpr * 16 + (2 * hrow) * 4 + (rem - own_rows * dpr)
    colk = iota((block, SLICES * 16), 1)
    for q in range(2):
        perm = jnp.where(colk == tgt + 4 * q, 1.0, 0.0).astype(BF)
        blk[:, 128 * q : 128 * (q + 1)] = dot32(perm, flat).astype(BF)

    def block_copy(k):
        return remote(blk, gath.at[c], a1s.at[k], a1q.at[c], at_column(k))

    def send_block(k, _):
        block_copy(lax.rem(c + k, cols)).start()
        return 0

    lax.fori_loop(1, cols, send_block, 0)
    gath[c] = blk[...]

    for k in range(1, SLICES):
        j = lax.rem(i + k, SLICES)
        remote(tabs.at[j], tabs.at[j], tbs.at[j], tbq.at[j], at_cube(j)).wait_recv()
    flat_tabs = tabs[...].reshape(SLICES * 8, 128)

    lm = iota((128, lanes), 1)
    cm = quotient(lm, block, lanes)
    rm = lm - block * cm
    hm = jnp.where(rm >= half, 1, 0)
    rm = rm - half * hm
    dm = quotient(rm, own_rows, half)
    tm = own_rows * cm + (rm - own_rows * dm)
    spread = jnp.where(iota((128, lanes), 0) == tm, 1.0, 0.0)
    wide = jnp.dot(flat_tabs, spread, precision=HIGH, preferred_element_type=F32)
    wide = jnp.where((iota((SLICES * 8, lanes), 0) >> 3) == dm[0 : SLICES * 8], wide, 0.0)
    wide = jnp.sum(wide.reshape(SLICES, 8, lanes), axis=0)
    slot_id = (iota((slots, lanes), 0) + 1).astype(F32)
    for h in range(2):
        for k in range(groups):
            key = jnp.where(hm[0:1] == h, wide[k : k + 1], 0.0)
            pick[h, k * slots : (k + 1) * slots, :] = jnp.where(
                slot_id == key, 1.0, 0.0
            ).astype(BF)

    mn = cols * half
    rows_m = iota((mn, 128), 0)
    cr = quotient(rows_m, half, mn)
    rr = rows_m - half * cr
    dr = quotient(rr, own_rows, half)
    tr = own_rows * cr + (rr - own_rows * dr)
    spread_t = jnp.where(iota((mn, 128), 1) == tr, 1.0, 0.0)
    tall = jnp.dot(spread_t, jnp.transpose(flat_tabs), precision=HIGH, preferred_element_type=F32)
    lane_t = iota((mn, SLICES * 8), 1)
    tall = jnp.where((lane_t >> 3) == dr[:, 0 : SLICES * 8], tall, 0.0)
    lane_w = iota((mn, zn * slots), 1)
    lz = quotient(lane_w, slots, zn * slots)
    slot_w = (lane_w - slots * lz + 1).astype(F32)
    lg = lz >> 1
    mix = jnp.zeros((mn, zn * slots), F32)
    for k in range(groups):
        key = jnp.sum(jnp.where((lane_t & 7) == k, tall, 0.0), axis=1, keepdims=True)
        wgt = jnp.sum(jnp.where((lane_t & 7) == 4 + k, tall, 0.0), axis=1, keepdims=True)
        mix = jnp.where((lg == k) & (slot_w == key), wgt, mix)
    mixw[...] = mix.astype(BF)

    def wait_block(k, _):
        j = lax.rem(c + k, cols)
        remote(blk, gath.at[j], a1s.at[j], a1q.at[j], at_column(j)).wait_recv()
        return 0

    lax.fori_loop(1, cols, wait_block, 0)

    tokens_all = gath[...].reshape(lanes, hw)
    for h in range(2):
        got = dot32(pick[h], tokens_all).astype(BF)
        sel[:, :, hw * h : hw * (h + 1)] = got.reshape(groups, slots, hw)

    def zmod(k):
        return lax.rem(z + k, zn)

    def out_copy(k):
        return remote(
            sel.at[lax.div(k, 2)], xb.at[p, zb, g], bzs.at[k], bzq.at[z], at_z(k)
        )

    far = [k for k in range(1, zn) if not (ring8 and k == 4)]
    for k in sorted(far, key=lambda k: -min(k, zn - k)):
        out_copy(zmod(k)).start()
    xb[p, zb, g] = sel[g]

    def in_z(k):
        ref = xb.at[p, lax.rem(k, 2), lax.div(k, 2)]
        return remote(ref, ref, bzs.at[k], bzq.at[k], at_z(k))

    def relay_copy(k):
        ref = xb.at[p, lax.rem(k, 2), lax.div(k, 2)]
        return remote(ref, ref, brs.at[0], bzq.at[k], at_z(z_mate_z))

    def x_copy(k, pos):
        ref = xb.at[pos, lax.rem(k, 2), lax.div(k, 2)]
        return remote(ref, ref, bxs.at[k], bxq.at[k], x_mate)

    def c_copy(k, pos, which):
        ref = xb.at[pos, lax.rem(k, 2), lax.div(k, 2)]
        return remote(ref, ref, bcs.at[which * zn + k], bcq.at[which * zn + k], core_mate)

    if ring8:
        kr = 5 - 2 * zb
        order = [0, 1, 7, kr, 2, 6, 8 - kr, 4]
    else:
        order = list(range(zn))
    for n, k in enumerate(order):
        src = zmod(k)
        if n > 0:
            in_z(src).wait_recv()
        if ring8 and n == 3:
            relay_copy(src).start()
        x_copy(src, p).start()
        c_copy(src, p, 0).start()

    loads[0].wait()
    loads[1].wait()

    def project(pos, first):
        for b in range(2):
            off = pl.multiple_of((b * 4 + pos) * sw, sw)
            part = xb[pos, b].reshape(groups * slots, sw)
            up = dot_rows(part, wu[:, pl.ds(off, sw)])
            gate = dot_rows(part, wg[:, pl.ds(off, sw)])
            if first and b == 0:
                acc[0] = gate
                acc[1] = up
            else:
                acc[0] += gate
                acc[1] += up

    project(p, True)
    for k in order:
        src = zmod(k)
        x_copy(src, px).wait_recv()
        c_copy(src, px, 1).start()
    project(px, False)
    pc = xl * 2 + (1 - core)
    pxc = (1 - xl) * 2 + (1 - core)
    for k in order:
        c_copy(zmod(k), pc, 0).wait_recv()
    project(pc, False)
    for k in order:
        c_copy(zmod(k), pxc, 1).wait_recv()
    project(pxc, False)

    gate = acc[0]
    hid[...] = (gate / (1.0 + jnp.exp(-gate)) * acc[1]).astype(BF)
    loads[2].wait()

    def down(b, pos):
        off = pl.multiple_of((b * 4 + pos) * sw, sw)
        return dot32(hid[...], wd[:, pl.ds(off, sw)]).reshape(groups, slots, sw)

    def pc_copy(which, b):
        return remote(
            pcs.at[which, b], pcr.at[which, b],
            dcs.at[2 * which + b], dcq.at[2 * which + b], core_mate,
        )

    def xd_copy(k):
        b, e = lax.rem(k, 2), lax.div(k, 2)
        return remote(xs.at[b, e], xr.at[b, e], dxs.at[k], dxq.at[k], x_mate)

    if ring8:
        back = [4, 8 - kr, kr, 2, 6, 1, 7, 0]
    else:
        back = list(range(zn - 1, -1, -1))
    for b in range(2):
        pcs[0, b] = down(b, pxc).astype(BF)
        pc_copy(0, b).start()
    for b in range(2):
        mine = down(b, px)
        pc_copy(0, b).wait_recv()
        xs[b] = (mine + pcr[0, b].astype(F32)).astype(BF)
    for k in back:
        xd_copy(zmod(k)).start()
    for b in range(2):
        pcs[1, b] = down(b, pc).astype(BF)
        pc_copy(1, b).start()
    for b in range(2):
        mine = down(b, p)
        pc_copy(1, b).wait_recv()
        own[b] = mine + pcr[1, b].astype(F32)

    def home_copy(k):
        return remote(zs.at[k], zr.at[z], dzs.at[k], dzq.at[z], at_z(k))

    def lent_copy():
        return remote(rls, rl, rss.at[0], rsq.at[0], at_z(z_mate_z))

    for n, k in enumerate(back):
        dst = zmod(k)
        b, e = lax.rem(dst, 2), lax.div(dst, 2)
        xd_copy(dst).wait_recv()
        total = own[b, e] + xr[b, e].astype(F32)
        if n == len(back) - 1:
            zr[z] = total.astype(BF)
        elif ring8 and n == 0:
            rls[...] = total.astype(BF)
            lent_copy().start()
        else:
            if ring8 and n == 2:
                lent_copy().wait_recv()
                total = total + rl[...].astype(F32)
            zs[dst] = total.astype(BF)
            home_copy(dst).start()
    if ring8:
        zr[zmod(4)] = jnp.zeros((slots, sw), BF)
    for n, k in enumerate(back[:-1]):
        if ring8 and n == 0:
            continue
        src = zmod(zn - k)
        remote(zs.at[src], zr.at[src], dzs.at[src], dzq.at[src], at_z(src)).wait_recv()

    for h in range(2):
        part = zr[:, :, hw * h : hw * (h + 1)].reshape(zn * slots, hw)
        es32[:, half * h : half * (h + 1), :] = dot32(mixw[...], part).reshape(cols, half, hw)
    es[...] = es32[...].astype(BF)

    def sum_copy(k):
        return remote(es.at[k], er.at[c], e1s.at[k], e1q.at[c], at_column(k))

    def send_sum(k, _):
        sum_copy(lax.rem(c + k, cols)).start()
        return 0

    lax.fori_loop(1, cols, send_sum, 0)
    er[c] = es[c]

    def wait_sum(k, _):
        j = lax.rem(c + k, cols)
        remote(es.at[j], er.at[j], e1s.at[j], e1q.at[j], at_column(j)).wait_recv()
        return 0

    lax.fori_loop(1, cols, wait_sum, 0)
    total = er[0].astype(F32)
    for k in range(1, cols):
        total = total + er[k].astype(F32)
    total = total.astype(BF)

    colb = iota((SLICES * 16, block), 1)
    hcol = jnp.where(colb >= half, 1, 0)
    rem = colb - half * hcol
    dpc = quotient(rem, own_rows, half)
    tgt = dpc * 16 + (2 * hcol) * 4 + (rem - own_rows * dpc)
    rowk = iota((SLICES * 16, block), 0)
    tiles = jnp.zeros((SLICES * 16, 128), F32)
    for q in range(2):
        perm = jnp.where(rowk == tgt + 4 * q, 1.0, 0.0).astype(BF)
        tiles = tiles + dot32(perm, total[:, 128 * q : 128 * (q + 1)])
    fin[...] = tiles.astype(BF).reshape(fin.shape)
    finr[i] = fin[i]

    for k in range(1, SLICES):
        j = lax.rem(i + k, SLICES)
        remote(fin.at[j], finr.at[i], e2s.at[j], e2q.at[i], at_cube(j)).start()
    for k in range(1, SLICES):
        j = lax.rem(i + k, SLICES)
        remote(fin.at[j], finr.at[j], e2s.at[j], e2q.at[j], at_cube(j)).wait_recv()
    stage32[...] = finr[...].astype(F32).reshape(SLICES * 16, 128)
    out_ref[...] = jnp.concatenate(
        [stage32[4 * k : 4 * k + own_rows, :] for k in range(SLICES * qn)], axis=1
    ).astype(BF)

    for k in range(1, SLICES):
        j = lax.rem(i + k, SLICES)
        slice_copy(j).wait_send()
        table_copy(j).wait_send()
        remote(fin.at[j], finr.at[i], e2s.at[j], e2q.at[i], at_cube(j)).wait_send()

    def wait_columns(k, _):
        j = lax.rem(c + k, cols)
        block_copy(j).wait_send()
        sum_copy(j).wait_send()
        return 0

    lax.fori_loop(1, cols, wait_columns, 0)
    for k in far:
        out_copy(zmod(k)).wait_send()
        home_copy(zmod(k)).wait_send()
    if ring8:
        relay_copy(zmod(kr)).wait_send()
        lent_copy().wait_send()
    for k in range(zn):
        x_copy(k, p).wait_send()
        c_copy(k, p, 0).wait_send()
        c_copy(k, px, 1).wait_send()
        xd_copy(k).wait_send()
    for which in range(2):
        for b in range(2):
            pc_copy(which, b).wait_send()


def local(tokens, expert_ids, gate_ints, gate_weight, up_weight, down_weight):
    groups = lax.axis_size("dp") // SLICES
    cols = lax.axis_size("expert")
    own_rows, width = tokens.shape
    hidden = gate_weight.shape[1]
    zn = 2 * groups
    sw = width // SLICES
    hw = sw // 2
    block = 2 * SLICES * own_rows
    half = SLICES * own_rows
    slots = SLICES * CAP
    vmem = pltpu.VMEM
    dma = pltpu.SemaphoreType.DMA
    sizes = (cols, groups, own_rows, width, hidden)
    scratch = [
        vmem((hidden, width), BF),
        vmem((hidden, width), BF),
        vmem((hidden, width), BF),
        vmem((SLICES * 16, 128), F32),
        vmem((SLICES, 16, 128), BF),
        vmem((SLICES, 16, 128), BF),
        vmem((SLICES, 8, 128), F32),
        vmem((block, hw), BF),
        vmem((cols, block, hw), BF),
        vmem((2, groups * slots, cols * block), BF),
        vmem((groups, slots, sw), BF),
        vmem((4, 2, groups, slots, sw), BF),
        vmem((2, groups * slots, hidden), F32),
        vmem((groups * slots, hidden), BF),
        vmem((2, 2, groups, slots, sw), BF),
        vmem((2, 2, groups, slots, sw), BF),
        vmem((2, groups, slots, sw), BF),
        vmem((2, groups, slots, sw), BF),
        vmem((2, groups, slots, sw), F32),
        vmem((zn, slots, sw), BF),
        vmem((zn, slots, sw), BF),
        vmem((slots, sw), BF),
        vmem((slots, sw), BF),
        vmem((cols * half, zn * slots), BF),
        vmem((cols, block, hw), F32),
        vmem((cols, block, hw), BF),
        vmem((cols, block, hw), BF),
        vmem((SLICES, 16, 128), BF),
        vmem((SLICES, 16, 128), BF),
        dma((3,)),
        dma((SLICES,)), dma((SLICES,)), dma((SLICES,)), dma((SLICES,)),
        dma((cols,)), dma((cols,)),
        dma((zn,)), dma((zn,)), dma((1,)),
        dma((zn,)), dma((zn,)), dma((2 * zn,)), dma((2 * zn,)),
        dma((4,)), dma((4,)), dma((zn,)), dma((zn,)),
        dma((zn,)), dma((zn,)), dma((1,)), dma((1,)),
        dma((cols,)), dma((cols,)), dma((SLICES,)), dma((SLICES,)),
    ]
    return pl.pallas_call(
        functools.partial(kernel, sizes),
        out_shape=jax.ShapeDtypeStruct((own_rows, width), BF),
        in_specs=[pl.BlockSpec(memory_space=pltpu.VMEM)] * 3
        + [pl.BlockSpec(memory_space=pl.ANY)] * 3,
        out_specs=pl.BlockSpec(memory_space=pltpu.VMEM),
        scratch_shapes=scratch,
        compiler_params=pltpu.CompilerParams(
            collective_id=0, has_side_effects=True, vmem_limit_bytes=56 * 1024 * 1024
        ),
    )(tokens, expert_ids, gate_ints, gate_weight, up_weight, down_weight)


def solution(mesh):
    return jax.shard_map(
        local,
        mesh=mesh,
        in_specs=(
            P(("dp", "expert"), None),
            P("dp", None),
            P("dp", None),
            P(("expert", "dp"), None, None),
            P(("expert", "dp"), None, None),
            P(("expert", "dp"), None, None),
        ),
        out_specs=P(("dp", "expert"), None),
        check_vma=False,
    )
```

time: 442 us -> 104 us (0.24); the launches traced: 433 us -> 102 us
  waiting for transfers between devices: 325 us -> 0 us
  Pallas kernels: 0 us -> 98.4 us
  blocking collectives: 38.1 us -> 0 us
  local copies, waits for them, and re-layouts: 34.6 us -> 4.12 us
  between operations: 14.2 us -> 0.01 us
  matrix products: 11.2 us -> 0 us
  starting transfers between devices: 5.69 us -> 0 us
  other arithmetic: 4.75 us -> 0 us
    unnamed x3 -> x0, waiting for transfers between devices: 147 us -> none
    pallas_call x0 -> x1, Pallas kernels: none -> 98.4 us  [local(): pl.pallas_call(functools.partial(kernel, sizes), out_shape=jax.ShapeDtype...]
    all_to_all x1 -> x0, waiting for transfers between devices: 94 us -> none  [local(): lax.all_to_all(parts, 'dp', split_axis=0, concat_axis=0, tiled=True)]
    all_gather x1 -> x0, waiting for transfers between devices: 83.4 us -> none  [local(): lax.all_gather(send_rows[None], 'dp', axis=0, tiled=True)]
    all_gather x1 -> x0, blocking collectives: 38.1 us -> none  [local(): gathered = lax.all_gather(tokens, 'expert', axis=0, tiled=True)]
    dynamic_slice x1 -> x0, local copies, waits for them, and re-layouts: 19.5 us -> none  [local(): lax.dynamic_index_in_dim(lax.all_gather(send_rows[None], 'dp', axis=0, ti...]
    dot_general x4 -> x0, matrix products: 11.2 us -> none  [the longest x1 6.03 us: expert_rows(): jnp.dot(hidden, w_down, preferred_element_type=jnp.float32)]
    reshape x5 -> x0, local copies, waits for them, and re-layouts: 9.56 us -> none  [the longest x1 4.66 us: expert_rows(): flat_rows = rows.reshape(-1, rows.shape[-1])]
  transfers between devices with their start and end apart: 3 -> 0, of which waited for: 3 -> 0; matrix products, arithmetic and copies ran while one was open for 0% -> 0% of each run, Pallas kernels for 0% -> 0%
where the time goes in v1:
time: 104 us; the launch traced here: 102 us
  Pallas kernels  98.4 us (95%)
  local copies, waits for them, and re-layouts  4.12 us (4%)
    pallas_call x1, Pallas kernels, local(): pl.pallas_call(functools.partial(kernel, sizes), out_shape=jax.ShapeDtype...  98.4 us
    unnamed x3, local copies, waits for them, and re-layouts  4.12 us

profile of v1, /device:TPU:1, one launch (start us, length us, event | category | flops | bytes accessed | tf_op | source)
XLA Modules:
  0.0 102.5 jit_solution(5781152338525009252)
XLA Ops:
  0.0 1.4 %copy.7.ids_ref = s32[48,8]{1,0:T(8,128)} copy(s32[48,8]{0,1:T(8,128)} %param.7) | data formatting | bytes 3072 | tf_op args[1]
  1.4 1.4 %copy.8.gates_ref = s32[48,8]{1,0:T(8,128)} copy(s32[48,8]{0,1:T(8,128)} %param.8) | data formatting | bytes 3072 | tf_op args[2]
  2.7 98.4 %shard_map.64 = bf16[3,4096]{1,0:T(4,128)(2,1)} custom-call(bf16[3,4096]{1,0:T(4,128)(2,1)} %tokens_ref.1, s32[48,8]{1,0:T(8,128)} %copy.7.ids_ref, s32[48,8]{1,0:T(8,128)} %copy.8.gates_ref, bf16[1,192,4096]{2,1,0:T(8,128)(2,1)} %wg_hbm.1, bf16[1,192,4096]{2,1,0:T(8,128)(2,1)} %wu_hbm.1, bf16[1,192,4096]{2,1,0:T(8,128)(2,1)} %wd_hbm.1), custom_call_target="tpu_custom_call" | custom-call | tf_op jit(solution)/shard_map/pallas_call | solution.py:500
  101.1 1.4 %copy.10 = bf16[3,4096]{1,0:T(4,128)(2,1)} copy(bf16[3,4096]{1,0:T(4,128)(2,1)} %shard_map.64) | data formatting | bytes 49152

commit v2 on v1

v2 whole, which is shorter than its diff:
```python
import functools

import jax
import jax.numpy as jnp
from jax import lax
from jax.experimental import pallas as pl
from jax.experimental.pallas import tpu as pltpu
from jax.sharding import PartitionSpec as P

SLICES = 8
CAP = 10
EARLY = 3
LATE = 6
BF = jnp.bfloat16
F32 = jnp.float32
HIGH = lax.Precision.HIGHEST


def quotient(x, n, top):
    mul = (1 << 16) // n + 1
    assert all((v * mul) >> 16 == v // n for v in range(top))
    return (x * mul) >> 16


def iota(shape, dim):
    return lax.broadcasted_iota(jnp.int32, shape, dim)


def dot32(a, b):
    return jnp.dot(a, b, preferred_element_type=F32)


def dot_rows(a, b):
    return lax.dot_general(a, b, (((1,), (1,)), ((), ())), preferred_element_type=F32)


def kernel(
    sizes, tokens_ref, ids_ref, gates_ref, wg_hbm, wu_hbm, wd_hbm, out_ref,
    wg, wu, wd, stage32, stage, a0r, tabs, blk, gath, pick, sel, xb, acc, hid,
    pcs, pcr, xs, xr, own, zs, zr, rl, rls, mixw, es32, es, er, fin, finr,
    wsem, a0s, a0q, tbs, tbq, a1s, a1q, bzs, bzq, brs, bxs, bxq, bcs, bcq,
    dcs, dcq, dxs, dxq, dzs, dzq, rss, rsq, e1s, e1q, e2s, e2q,
):
    cols, groups, own_rows, width, hidden = sizes
    zn = 2 * groups
    sw = width // SLICES
    hw = sw // 2
    qn = sw // 128
    block = 2 * SLICES * own_rows
    half = SLICES * own_rows
    slots = SLICES * CAP
    lanes = cols * block
    ring8 = zn == 8

    d = lax.axis_index("dp")
    c = lax.axis_index("expert")
    g = lax.div(d, SLICES)
    i = lax.rem(d, SLICES)
    zb = lax.div(i, 4)
    xl = lax.rem(lax.div(i, 2), 2)
    core = lax.rem(i, 2)
    z = 2 * g + zb
    p = xl * 2 + core
    px = (1 - xl) * 2 + core

    def at_cube(j):
        return {"dp": g * SLICES + j, "expert": c}

    def at_column(k):
        return {"dp": d, "expert": k}

    def at_z(k):
        return {"dp": k * 4 + p, "expert": c}

    x_mate = {"dp": z * 4 + px, "expert": c}
    core_mate = {"dp": z * 4 + xl * 2 + (1 - core), "expert": c}
    z_mate_z = 2 * g + (1 - zb)

    def remote(src, dst, ssem, rsem, dev):
        return pltpu.make_async_remote_copy(
            src_ref=src, dst_ref=dst, send_sem=ssem, recv_sem=rsem,
            device_id=dev, device_id_type=pl.DeviceIdType.MESH,
        )

    sent = []

    def start(copy):
        copy.start()
        sent.append(copy)

    def finish():
        for copy in sent:
            copy.wait_send()

    loads = [
        pltpu.make_async_copy(wg_hbm.at[0], wg, wsem.at[0]),
        pltpu.make_async_copy(wu_hbm.at[0], wu, wsem.at[1]),
        pltpu.make_async_copy(wd_hbm.at[0], wd, wsem.at[2]),
    ]
    for load in loads:
        load.start()

    barrier = pltpu.get_barrier_semaphore()

    def signal(dev):
        pl.semaphore_signal(barrier, inc=1, device_id=dev, device_id_type=pl.DeviceIdType.MESH)

    for k in range(1, SLICES):
        signal(at_cube(lax.rem(i + k, SLICES)))
    for k in range(1, cols):
        signal(at_column(lax.rem(c + k, cols)))
    for k in range(1, groups):
        other = lax.rem(g + k, groups)
        signal(at_z(2 * other))
        signal(at_z(2 * other + 1))

    tok = tokens_ref[...].astype(F32)
    stage32[...] = jnp.zeros_like(stage32)
    for k in range(SLICES * qn):
        stage32[4 * k : 4 * k + own_rows, :] = tok[:, 128 * k : 128 * (k + 1)]
    stage[...] = stage32[...].astype(BF).reshape(stage.shape)

    ids = ids_ref[...]
    gates = gates_ref[...].astype(F32)
    shares = gates / jnp.sum(gates, axis=0, keepdims=True)
    rows = ids.shape[1]
    line = iota((8, rows), 0)
    cat = jnp.zeros((8, rows), F32)
    for k in range(groups):
        hit = ids == c * groups + k
        named = jnp.sum(jnp.where(hit, 1.0, 0.0), axis=0, keepdims=True)
        weight = jnp.sum(jnp.where(hit, shares, 0.0), axis=0, keepdims=True)
        cat = jnp.where(line == k, named, cat)
        cat = jnp.where(line == 4 + k, weight, cat)
    upper = jnp.where(iota((rows, rows), 0) < iota((rows, rows), 1), 1.0, 0.0)
    rank = dot32(cat.astype(BF), upper.astype(BF))
    base = (i * CAP + 1).astype(F32)
    table = jnp.where(line < 4, jnp.where(cat > 0.0, rank + base, 0.0), cat)
    tabs[i] = jnp.concatenate([table, jnp.zeros((8, 128 - rows), F32)], axis=1)
    a0r[i] = stage[i]

    pl.semaphore_wait(barrier, SLICES - 1 + cols - 1 + zn - 2)

    def slice_copy(j):
        return remote(stage.at[j], a0r.at[i], a0s.at[j], a0q.at[i], at_cube(j))

    def table_copy(j):
        return remote(tabs.at[i], tabs.at[i], tbs.at[j], tbq.at[i], at_cube(j))

    for k in range(1, SLICES):
        start(slice_copy(lax.rem(i + k, SLICES)))
    for k in range(1, SLICES):
        start(table_copy(lax.rem(i + k, SLICES)))
    for k in range(1, SLICES):
        j = lax.rem(i + k, SLICES)
        remote(stage.at[j], a0r.at[j], a0s.at[j], a0q.at[j], at_cube(j)).wait_recv()

    flat = a0r[...].reshape(SLICES * 16, 128)
    row = iota((block, SLICES * 16), 0)
    hrow = jnp.where(row >= half, 1, 0)
    rem = row - half * hrow
    dpr = quotient(rem, own_rows, half)
    tgt = dpr * 16 + hrow * 4 + (rem - own_rows * dpr)
    colk = iota((block, SLICES * 16), 1)

    def block_copy(k, t):
        return remote(blk.at[t], gath.at[t, c], a1s.at[t, k], a1q.at[t, c], at_column(k))

    for t in range(2):
        perm = jnp.where(colk == tgt + 8 * t, 1.0, 0.0).astype(BF)
        blk[t] = dot32(perm, flat).astype(BF)
        for k in range(1, cols):
            start(block_copy(lax.rem(c + k, cols), t))
        gath[t, c] = blk[t]

    for k in range(1, SLICES):
        j = lax.rem(i + k, SLICES)
        remote(tabs.at[j], tabs.at[j], tbs.at[j], tbq.at[j], at_cube(j)).wait_recv()
    flat_tabs = tabs[...].reshape(SLICES * 8, 128)

    lm = iota((128, lanes), 1)
    cm = quotient(lm, block, lanes)
    rm = lm - block * cm
    hm = jnp.where(rm >= half, 1, 0)
    rm = rm - half * hm
    dm = quotient(rm, own_rows, half)
    tm = own_rows * cm + (rm - own_rows * dm)
    spread = jnp.where(iota((128, lanes), 0) == tm, 1.0, 0.0)
    wide = jnp.dot(flat_tabs, spread, precision=HIGH, preferred_element_type=F32)
    wide = jnp.where((iota((SLICES * 8, lanes), 0) >> 3) == dm[0 : SLICES * 8], wide, 0.0)
    wide = jnp.sum(wide.reshape(SLICES, 8, lanes), axis=0)
    slot_id = (iota((slots, lanes), 0) + 1).astype(F32)
    for h in range(2):
        for k in range(groups):
            key = jnp.where(hm[0:1] == h, wide[k : k + 1], 0.0)
            pick[h, k * slots : (k + 1) * slots, :] = jnp.where(
                slot_id == key, 1.0, 0.0
            ).astype(BF)

    def make_mix():
        mn = cols * half
        rows_m = iota((mn, 128), 0)
        cr = quotient(rows_m, half, mn)
        rr = rows_m - half * cr
        dr = quotient(rr, own_rows, half)
        tr = own_rows * cr + (rr - own_rows * dr)
        spread_t = jnp.where(iota((mn, 128), 1) == tr, 1.0, 0.0)
        tall = jnp.dot(spread_t, jnp.transpose(flat_tabs), precision=HIGH, preferred_element_type=F32)
        lane_t = iota((mn, SLICES * 8), 1)
        tall = jnp.where((lane_t >> 3) == dr[:, 0 : SLICES * 8], tall, 0.0)
        lane_w = iota((mn, zn * slots), 1)
        lz = quotient(lane_w, slots, zn * slots)
        slot_w = (lane_w - slots * lz + 1).astype(F32)
        lg = lz >> 1
        mix = jnp.zeros((mn, zn * slots), F32)
        for k in range(groups):
            key = jnp.sum(jnp.where((lane_t & 7) == k, tall, 0.0), axis=1, keepdims=True)
            wgt = jnp.sum(jnp.where((lane_t & 7) == 4 + k, tall, 0.0), axis=1, keepdims=True)
            mix = jnp.where((lg == k) & (slot_w == key), wgt, mix)
        mixw[...] = mix.astype(BF)

    def zmod(k):
        return lax.rem(z + k, zn)

    def out_copy(k, t):
        return remote(
            sel.at[t, lax.div(k, 2)], xb.at[t, p, zb, g], bzs.at[t, k], bzq.at[t, z], at_z(k)
        )

    def spot(k, pos, t):
        return xb.at[t, pos, lax.rem(k, 2), lax.div(k, 2)]

    def in_z(k, t):
        ref = spot(k, p, t)
        return remote(ref, ref, bzs.at[t, k], bzq.at[t, k], at_z(k))

    def relay_copy(k, t):
        ref = spot(k, p, t)
        return remote(ref, ref, brs.at[t], bzq.at[t, k], at_z(z_mate_z))

    def x_copy(k, pos, t):
        ref = spot(k, pos, t)
        return remote(ref, ref, bxs.at[t, k], bxq.at[t, k], x_mate)

    def c_copy(k, pos, which, t):
        ref = spot(k, pos, t)
        return remote(ref, ref, bcs.at[t, which * zn + k], bcq.at[t, which * zn + k], core_mate)

    if ring8:
        kr = 5 - 2 * zb
        order = [0, 1, 7, kr, 2, 6, 8 - kr, 4]
        leave = order[1:7]
    else:
        order = list(range(zn))
        leave = order[1:]

    def pass_on(k, t):
        start(x_copy(k, p, t))
        start(c_copy(k, p, 0, t))

    def dispatch(t):
        def wait_block(k, _):
            j = lax.rem(c + k, cols)
            remote(
                blk.at[t], gath.at[t, j], a1s.at[t, j], a1q.at[t, j], at_column(j)
            ).wait_recv()
            return 0

        lax.fori_loop(1, cols, wait_block, 0)
        tokens_all = gath[t].reshape(lanes, 128)
        for h in range(2):
            got = dot32(pick[h], tokens_all).astype(BF)
            sel[t, :, :, 128 * h : 128 * (h + 1)] = got.reshape(groups, slots, 128)
        for k in leave:
            start(out_copy(zmod(k), t))
        xb[t, p, zb, g] = sel[t, g]
        pass_on(z, t)

    def arrive(n, t):
        src = zmod(order[n])
        in_z(src, t).wait_recv()
        if ring8 and n == 3:
            start(relay_copy(src, t))
        pass_on(src, t)

    early = EARLY if ring8 else 1
    dispatch(0)
    for n in range(1, early):
        arrive(n, 0)
    dispatch(1)
    for n in range(early, zn):
        arrive(n, 0)

    loads[0].wait()
    loads[1].wait()

    def project(pos, t, first=False):
        for b in range(2):
            off = pl.multiple_of((b * 4 + pos) * sw + t * hw, hw)
            part = xb[t, pos, b].reshape(groups * slots, hw)
            up = dot_rows(part, wu[:, pl.ds(off, hw)])
            gate = dot_rows(part, wg[:, pl.ds(off, hw)])
            if first and b == 0:
                acc[0] = gate
                acc[1] = up
            else:
                acc[0] += gate
                acc[1] += up

    pc = xl * 2 + (1 - core)
    pxc = (1 - xl) * 2 + (1 - core)

    def cross(n, t):
        src = zmod(order[n])
        x_copy(src, px, t).wait_recv()
        start(c_copy(src, px, 1, t))

    def wait_core(pos, which, t):
        for k in range(zn):
            c_copy(k, pos, which, t).wait_recv()

    for n in range(1, zn):
        arrive(n, 1)
    for n in range(zn):
        cross(n, 0)
    project(p, 0, True)
    project(p, 1)
    for n in range(zn // 2):
        cross(n, 1)
    project(px, 0)
    wait_core(pc, 0, 0)
    project(pc, 0)
    make_mix()
    for n in range(zn // 2, zn):
        cross(n, 1)
    wait_core(pxc, 1, 0)
    project(pxc, 0)
    project(px, 1)
    wait_core(pc, 0, 1)
    project(pc, 1)
    wait_core(pxc, 1, 1)
    project(pxc, 1)

    gate = acc[0]
    hid[...] = (gate / (1.0 + jnp.exp(-gate)) * acc[1]).astype(BF)
    loads[2].wait()

    def down(b, pos, t):
        off = pl.multiple_of((b * 4 + pos) * sw + t * hw, hw)
        return dot32(hid[...], wd[:, pl.ds(off, hw)]).reshape(groups, slots, hw)

    def pc_copy(which, b, t):
        n = 4 * which + 2 * t + b
        return remote(pcs.at[which, t, b], pcr.at[which, t, b], dcs.at[n], dcq.at[n], core_mate)

    def xd_copy(k, t):
        b, e = lax.rem(k, 2), lax.div(k, 2)
        return remote(xs.at[t, b, e], xr.at[t, b, e], dxs.at[t, k], dxq.at[t, k], x_mate)

    if ring8:
        back = [4, 8 - kr, kr, 2, 6, 1, 7, 0]
    else:
        back = list(range(zn - 1, -1, -1))
    for t in range(2):
        for b in range(2):
            pcs[0, t, b] = down(b, pxc, t).astype(BF)
            start(pc_copy(0, b, t))
    for t in range(2):
        for b in range(2):
            mine = down(b, px, t)
            pc_copy(0, b, t).wait_recv()
            xs[t, b] = (mine + pcr[0, t, b].astype(F32)).astype(BF)
        for k in back:
            start(xd_copy(zmod(k), t))
    for t in range(2):
        for b in range(2):
            pcs[1, t, b] = down(b, pc, t).astype(BF)
            start(pc_copy(1, b, t))
    for t in range(2):
        for b in range(2):
            mine = down(b, p, t)
            pc_copy(1, b, t).wait_recv()
            own[t, b] = mine + pcr[1, t, b].astype(F32)

    def home_copy(k, t):
        return remote(zs.at[t, k], zr.at[t, z], dzs.at[t, k], dzq.at[t, z], at_z(k))

    def lent_copy(t):
        return remote(rls.at[t], rl.at[t], rss.at[t], rsq.at[t], at_z(z_mate_z))

    def give_back(n, t):
        dst = zmod(back[n])
        b, e = lax.rem(dst, 2), lax.div(dst, 2)
        xd_copy(dst, t).wait_recv()
        total = own[t, b, e] + xr[t, b, e].astype(F32)
        if n == zn - 1:
            zr[t, z] = total.astype(BF)
        elif ring8 and n == 0:
            rls[t] = total.astype(BF)
            start(lent_copy(t))
        else:
            if ring8 and n == 2:
                lent_copy(t).wait_recv()
                total = total + rl[t].astype(F32)
            zs[t, dst] = total.astype(BF)
            start(home_copy(dst, t))

    def sum_copy(k, t):
        return remote(es.at[t, k], er.at[t, c], e1s.at[t, k], e1q.at[t, c], at_column(k))

    def settle(t):
        if ring8:
            zr[t, zmod(4)] = jnp.zeros((slots, hw), BF)
        for n, k in enumerate(back[:-1]):
            if ring8 and n == 0:
                continue
            src = zmod(zn - k)
            remote(
                zs.at[t, src], zr.at[t, src], dzs.at[t, src], dzq.at[t, src], at_z(src)
            ).wait_recv()
        mixed = dot32(mixw[...], zr[t].reshape(zn * slots, hw))
        for h in range(2):
            es32[:, half * h : half * (h + 1), :] = mixed[:, 128 * h : 128 * (h + 1)].reshape(
                cols, half, 128
            )
        es[t] = es32[...].astype(BF)
        for k in range(1, cols):
            start(sum_copy(lax.rem(c + k, cols), t))
        er[t, c] = es[t, c]

    for n in range(zn):
        give_back(n, 0)
    late = LATE if ring8 else zn - 1
    for n in range(late):
        give_back(n, 1)
    settle(0)
    for n in range(late, zn):
        give_back(n, 1)
    settle(1)

    def column_sum(t):
        def wait_sum(k, _):
            j = lax.rem(c + k, cols)
            remote(
                es.at[t, j], er.at[t, j], e1s.at[t, j], e1q.at[t, j], at_column(j)
            ).wait_recv()
            return 0

        lax.fori_loop(1, cols, wait_sum, 0)
        total = er[t, 0].astype(F32)
        for k in range(1, cols):
            total = total + er[t, k].astype(F32)
        return total.astype(BF)

    colb = iota((SLICES * 16, block), 1)
    hcol = jnp.where(colb >= half, 1, 0)
    rem = colb - half * hcol
    dpc = quotient(rem, own_rows, half)
    tgt = dpc * 16 + hcol * 4 + (rem - own_rows * dpc)
    rowk = iota((SLICES * 16, block), 0)
    tiles = jnp.zeros((SLICES * 16, 128), F32)
    for t in range(2):
        perm = jnp.where(rowk == tgt + 8 * t, 1.0, 0.0).astype(BF)
        tiles = tiles + dot32(perm, column_sum(t))
    fin[...] = tiles.astype(BF).reshape(fin.shape)
    finr[i] = fin[i]

    for k in range(1, SLICES):
        j = lax.rem(i + k, SLICES)
        start(remote(fin.at[j], finr.at[i], e2s.at[j], e2q.at[i], at_cube(j)))
    for k in range(1, SLICES):
        j = lax.rem(i + k, SLICES)
        remote(fin.at[j], finr.at[j], e2s.at[j], e2q.at[j], at_cube(j)).wait_recv()
    stage32[...] = finr[...].astype(F32).reshape(SLICES * 16, 128)
    out_ref[...] = jnp.concatenate(
        [stage32[4 * k : 4 * k + own_rows, :] for k in range(SLICES * qn)], axis=1
    ).astype(BF)

    finish()


def local(tokens, expert_ids, gate_ints, gate_weight, up_weight, down_weight):
    groups = lax.axis_size("dp") // SLICES
    cols = lax.axis_size("expert")
    own_rows, width = tokens.shape
    hidden = gate_weight.shape[1]
    zn = 2 * groups
    sw = width // SLICES
    hw = sw // 2
    block = 2 * SLICES * own_rows
    half = SLICES * own_rows
    slots = SLICES * CAP
    vmem = pltpu.VMEM
    dma = pltpu.SemaphoreType.DMA
    sizes = (cols, groups, own_rows, width, hidden)
    scratch = [
        vmem((hidden, width), BF),
        vmem((hidden, width), BF),
        vmem((hidden, width), BF),
        vmem((SLICES * 16, 128), F32),
        vmem((SLICES, 16, 128), BF),
        vmem((SLICES, 16, 128), BF),
        vmem((SLICES, 8, 128), F32),
        vmem((2, block, 128), BF),
        vmem((2, cols, block, 128), BF),
        vmem((2, groups * slots, cols * block), BF),
        vmem((2, groups, slots, hw), BF),
        vmem((2, 4, 2, groups, slots, hw), BF),
        vmem((2, groups * slots, hidden), F32),
        vmem((groups * slots, hidden), BF),
        vmem((2, 2, 2, groups, slots, hw), BF),
        vmem((2, 2, 2, groups, slots, hw), BF),
        vmem((2, 2, groups, slots, hw), BF),
        vmem((2, 2, groups, slots, hw), BF),
        vmem((2, 2, groups, slots, hw), F32),
        vmem((2, zn, slots, hw), BF),
        vmem((2, zn, slots, hw), BF),
        vmem((2, slots, hw), BF),
        vmem((2, slots, hw), BF),
        vmem((cols * half, zn * slots), BF),
        vmem((cols, block, 128), F32),
        vmem((2, cols, block, 128), BF),
        vmem((2, cols, block, 128), BF),
        vmem((SLICES, 16, 128), BF),
        vmem((SLICES, 16, 128), BF),
        dma((3,)),
        dma((SLICES,)), dma((SLICES,)), dma((SLICES,)), dma((SLICES,)),
        dma((2, cols)), dma((2, cols)),
        dma((2, zn)), dma((2, zn)), dma((2,)),
        dma((2, zn)), dma((2, zn)), dma((2, 2 * zn)), dma((2, 2 * zn)),
        dma((8,)), dma((8,)), dma((2, zn)), dma((2, zn)),
        dma((2, zn)), dma((2, zn)), dma((2,)), dma((2,)),
        dma((2, cols)), dma((2, cols)), dma((SLICES,)), dma((SLICES,)),
    ]
    return pl.pallas_call(
        functools.partial(kernel, sizes),
        out_shape=jax.ShapeDtypeStruct((own_rows, width), BF),
        in_specs=[pl.BlockSpec(memory_space=pltpu.VMEM)] * 3
        + [pl.BlockSpec(memory_space=pl.ANY)] * 3,
        out_specs=pl.BlockSpec(memory_space=pltpu.VMEM),
        scratch_shapes=scratch,
        compiler_params=pltpu.CompilerParams(
            collective_id=0, has_side_effects=True, vmem_limit_bytes=56 * 1024 * 1024
        ),
    )(tokens, expert_ids.T, gate_ints.T, gate_weight, up_weight, down_weight)


def solution(mesh):
    return jax.shard_map(
        local,
        mesh=mesh,
        in_specs=(
            P(("dp", "expert"), None),
            P("dp", None),
            P("dp", None),
            P(("expert", "dp"), None, None),
            P(("expert", "dp"), None, None),
            P(("expert", "dp"), None, None),
        ),
        out_specs=P(("dp", "expert"), None),
        check_vma=False,
    )
```

time: 104 us -> 90 us (0.87); the launches traced: 102 us -> 89.7 us
  Pallas kernels: 98.4 us -> 88.3 us
  local copies, waits for them, and re-layouts: 4.12 us -> 1.39 us
    pallas_call x1, Pallas kernels: 98.4 us -> 88.3 us  [local(): pl.pallas_call(functools.partial(kernel, sizes), out_shape=jax.ShapeDtype...]
    unnamed x3 -> x1, local copies, waits for them, and re-layouts: 4.12 us -> 1.39 us
where the time goes in v2:
time: 90 us; the launch traced here: 89.7 us
  Pallas kernels  88.3 us (98%)
  local copies, waits for them, and re-layouts  1.39 us (2%)
    pallas_call x1, Pallas kernels, local(): pl.pallas_call(functools.partial(kernel, sizes), out_shape=jax.ShapeDtype...  88.3 us

profile of v2, /device:TPU:1, one launch (start us, length us, event | category | flops | bytes accessed | tf_op | source)
XLA Modules:
  0.0 89.7 jit_solution(18121242444924531127)
XLA Ops:
  0.0 88.3 %shard_map.64 = bf16[3,4096]{1,0:T(4,128)(2,1)} custom-call(bf16[3,4096]{1,0:T(4,128)(2,1)} %tokens_ref.1, s32[8,48]{1,0:T(8,128)} %bitcast.2, s32[8,48]{1,0:T(8,128)} %bitcast.3, bf16[1,192,4096]{2,1,0:T(8,128)(2,1)} %wg_hbm.1, bf16[1,192,4096]{2,1,0:T(8,128)(2,1)} %wu_hbm.1, bf16[1,192,4096]{2,1,0:T(8,128)(2,1)} %wd_hbm.1), custom_call_target="tpu_custom_call" | custom-call | tf_op jit(solution)/shard_map/pallas_call | solution.py:535
  88.3 1.4 %copy.8 = bf16[3,4096]{1,0:T(4,128)(2,1)} copy(bf16[3,4096]{1,0:T(4,128)(2,1)} %shard_map.64) | data formatting | bytes 49152

commit v3 on v2

--- a/solution.py
+++ b/solution.py
@@ -88,9 +88,11 @@
         copy.start()
         sent.append(copy)
 
-    def finish():
-        for copy in sent:
+    def finish(keep=0):
+        done = len(sent) - keep
+        for copy in sent[:done]:
             copy.wait_send()
+        del sent[:done]
 
     loads = [
         pltpu.make_async_copy(wg_hbm.at[0], wg, wsem.at[0]),
@@ -219,6 +221,8 @@
             mix = jnp.where((lg == k) & (slot_w == key), wgt, mix)
         mixw[...] = mix.astype(BF)
 
+    make_mix()
+
     def zmod(k):
         return lax.rem(z + k, zn)
 
@@ -282,17 +286,6 @@
         if ring8 and n == 3:
             start(relay_copy(src, t))
         pass_on(src, t)
-
-    early = EARLY if ring8 else 1
-    dispatch(0)
-    for n in range(1, early):
-        arrive(n, 0)
-    dispatch(1)
-    for n in range(early, zn):
-        arrive(n, 0)
-
-    loads[0].wait()
-    loads[1].wait()
 
     def project(pos, t, first=False):
         for b in range(2):
@@ -319,25 +312,37 @@
         for k in range(zn):
             c_copy(k, pos, which, t).wait_recv()
 
-    for n in range(1, zn):
+    early, mid = min(EARLY, zn), zn // 2
+    dispatch(0)
+    for n in range(1, early):
+        arrive(n, 0)
+    dispatch(1)
+    for n in range(early, zn):
+        arrive(n, 0)
+    loads[0].wait()
+    loads[1].wait()
+    project(p, 0, True)
+    for n in range(1, mid + 1):
         arrive(n, 1)
-    for n in range(zn):
+    for n in range(mid):
         cross(n, 0)
-    project(p, 0, True)
-    project(p, 1)
-    for n in range(zn // 2):
-        cross(n, 1)
-    project(px, 0)
     wait_core(pc, 0, 0)
     project(pc, 0)
-    make_mix()
-    for n in range(zn // 2, zn):
+    for n in range(mid + 1, zn):
+        arrive(n, 1)
+    for n in range(mid, zn):
+        cross(n, 0)
+    project(p, 1)
+    project(px, 0)
+    for n in range(mid):
         cross(n, 1)
+    wait_core(pc, 0, 1)
+    project(pc, 1)
     wait_core(pxc, 1, 0)
     project(pxc, 0)
+    for n in range(mid, zn):
+        cross(n, 1)
     project(px, 1)
-    wait_core(pc, 0, 1)
-    project(pc, 1)
     wait_core(pxc, 1, 1)
     project(pxc, 1)
 
@@ -437,6 +442,7 @@
     for n in range(late, zn):
         give_back(n, 1)
     settle(1)
+    finish(cols - 1)
 
     def column_sum(t):
         def wait_sum(k, _):

time: 90 us -> 89.6 us (level)
  no operation moved by 1% of the time
where the time goes in v3:
time: 89.6 us; the launch traced here: 89.4 us
  Pallas kernels  88 us (98%)
  local copies, waits for them, and re-layouts  1.39 us (2%)
    pallas_call x1, Pallas kernels, local(): pl.pallas_call(functools.partial(kernel, sizes), out_shape=jax.ShapeDtype...  88 us

profile of v3, /device:TPU:1, one launch (start us, length us, event | category | flops | bytes accessed | tf_op | source)
XLA Modules:
  0.0 89.4 jit_solution(7402021354549869317)
XLA Ops:
  0.0 88.0 %shard_map.64 = bf16[3,4096]{1,0:T(4,128)(2,1)} custom-call(bf16[3,4096]{1,0:T(4,128)(2,1)} %tokens_ref.1, s32[8,48]{1,0:T(8,128)} %bitcast.2, s32[8,48]{1,0:T(8,128)} %bitcast.3, bf16[1,192,4096]{2,1,0:T(8,128)(2,1)} %wg_hbm.1, bf16[1,192,4096]{2,1,0:T(8,128)(2,1)} %wu_hbm.1, bf16[1,192,4096]{2,1,0:T(8,128)(2,1)} %wd_hbm.1), custom_call_target="tpu_custom_call" | custom-call | tf_op jit(solution)/shard_map/pallas_call | solution.py:541
  88.0 1.4 %copy.8 = bf16[3,4096]{1,0:T(4,128)(2,1)} copy(bf16[3,4096]{1,0:T(4,128)(2,1)} %shard_map.64) | data formatting | bytes 49152
